TPU v7x, 32 devices: a whole 2x2x4 slice. The times are simulated.
32 devices in a mesh: batch: 8 (over z, x), tensor: 4 (over y, core).
Axes of the slice: x: 2, y: 2, z: 4, core: 2. Of those that a mesh axis runs over, the one named last changes fastest.
Arguments:
- fresh_hidden_state: bfloat16 [256, 3, 8192], P('batch', None, 'tensor'), may hold values from -6 to 6
- base_query_rows: bfloat16 [256, 3, 8192], P('batch', None, 'tensor'), may hold values from -8 to 8
- fresh_key_rows: bfloat16 [256, 3, 1024], P('batch', None, 'tensor'), may hold values from -6 to 6
- fresh_value_rows: bfloat16 [256, 3, 1024], P('batch', None, 'tensor'), may hold values from -12 to 12
- context_key_cache: bfloat16 [256, 64, 1024], P('batch', None, 'tensor'), may hold values from -6 to 6
- context_value_cache: bfloat16 [256, 64, 1024], P('batch', None, 'tensor'), may hold values from -12 to 12
- document_key_rows: bfloat16 [16, 512, 1024], P('batch', None, 'tensor'), may hold values from -6 to 6
- document_value_rows: bfloat16 [16, 512, 1024], P('batch', None, 'tensor'), may hold values from -12 to 12
- adapter_down_panel: bfloat16 [16, 64, 8192], P('batch', None, 'tensor'), may hold values from -0.0625 to 0.0625
- adapter_up_panel: bfloat16 [16, 64, 8192], P('batch', None, 'tensor'), may hold values from -0.75 to 0.75
- tenant_owner_batch: int32 [256, 1], P('batch'), may hold values from 0 to 7; in each aligned block of 32 rows (0 to 31, 32 to 63, ...) at most 8 rows name the same one
- tenant_local_index: int32 [256], P('batch'), may hold values from 0 to 1
- document_block_count: int32 [16], P('batch'), may hold values from 1 to 4, as said below
Outputs:
- attention: bfloat16 [256, 3, 8192], P('batch', None, 'tensor')
Inputs may be any that keep to these rules, and one draw needn't show every extreme that they name: `tenant_owner_batch`: among the 32 requests of one index of batch, at most 8 name the same owner, and in every draw some owner is named by exactly 8 of them. `document_block_count`: some tenant's document has exactly 4 blocks.
All inputs are finite; a program needn't handle non-finite values.
Results may differ from a plain program's by a relative error of at most 0.0064.
Values may be sent and summed in bfloat16 or wider, within the bound.
A program may use at most 128 MiB of HBM per device.

v0:
```python
import jax
import jax.numpy as jnp
from jax import lax
from jax.sharding import PartitionSpec as P

HEAD_SIZE = 128
DOC_BLOCK = 128


def local(
    fresh_hidden_state,
    base_query_rows,
    fresh_key_rows,
    fresh_value_rows,
    context_key_cache,
    context_value_cache,
    document_key_rows,
    document_value_rows,
    adapter_down_panel,
    adapter_up_panel,
    tenant_owner_batch,
    tenant_local_index,
    document_block_count,
):
    requests, steps_all, local_width_span = fresh_hidden_state.shape
    head_column_span = base_query_rows.shape[2]
    kv_cols = fresh_key_rows.shape[2]
    kv_heads = kv_cols // HEAD_SIZE
    head_count = head_column_span // HEAD_SIZE
    group_size = head_count // kv_heads
    owners = lax.axis_size("batch")
    capacity = max(2, 2 * requests // owners)
    tenant_list = adapter_down_panel.shape[0]
    rank_weight_width = adapter_down_panel.shape[1]
    doc_len = document_key_rows.shape[1]
    ctx_len = context_key_cache.shape[1]
    score_scale = HEAD_SIZE ** (-0.5)
    owner_of = tenant_owner_batch[:, 0]
    position = jnp.arange(requests)
    earlier = (owner_of[:, None] == owner_of[None, :]) & (position[None, :] < position[:, None])
    slot_index = owner_of * capacity + jnp.sum(earlier.astype(jnp.int32), axis=1)
    down_panels_every = adapter_down_panel.reshape(
        tenant_list * rank_weight_width, local_width_span
    )
    up_panels_every = adapter_up_panel.reshape(tenant_list * rank_weight_width, head_column_span)
    doc_k = document_key_rows.reshape(tenant_list * doc_len, kv_heads, HEAD_SIZE)
    doc_v = document_value_rows.reshape(tenant_list * doc_len, kv_heads, HEAD_SIZE)
    key_range = jnp.arange(tenant_list * doc_len)
    key_tenant = (key_range // doc_len).astype(jnp.float32)
    key_open = key_range % doc_len < jnp.repeat(
        DOC_BLOCK * document_block_count, doc_len, total_repeat_length=tenant_list * doc_len
    )
    tenant_ids = jnp.arange(tenant_list).astype(jnp.float32)
    keys_all = jnp.concatenate([context_key_cache, fresh_key_rows], axis=1)
    values_all = jnp.concatenate([context_value_cache, fresh_value_rows], axis=1)

    def attend_doc(block_in):
        q_rows, t_rows = block_in
        block_rows = q_rows.shape[0]
        query_head_rows = q_rows.reshape(block_rows, kv_heads, group_size, HEAD_SIZE)
        scores = (
            jnp.einsum("nkgd,mkd->nkgm", query_head_rows, doc_k, preferred_element_type=jnp.float32)
            * score_scale
        )
        is_valid = (t_rows[:, None] == key_tenant[None, :]) & key_open[None, :]
        scores = jnp.where(is_valid[:, None, None, :], scores, -jnp.inf)
        row_peak = jnp.max(scores, axis=-1)
        weights = jnp.exp(scores - row_peak[..., None]).astype(jnp.bfloat16)
        row_total = jnp.sum(weights, axis=-1, dtype=jnp.float32)
        mixed_out = jnp.einsum("nkgm,mkd->nkgd", weights, doc_v, preferred_element_type=jnp.float32)
        return (
            mixed_out.reshape(block_rows, head_column_span),
            row_peak.reshape(block_rows, head_count),
            row_total.reshape(block_rows, head_count),
        )

    outputs = []
    for decode_step_index in range(steps_all):
        step_from = decode_step_index
        step_upto = decode_step_index + 1
        width_steps = step_upto - step_from

        def place(value_rows_list):
            buffer = jnp.zeros(
                (owners * capacity, width_steps, value_rows_list.shape[2]), value_rows_list.dtype
            )
            return (
                buffer.at[slot_index]
                .set(value_rows_list[:, step_from:step_upto])
                .reshape(owners, capacity, width_steps, value_rows_list.shape[2])
            )

        which_tenant = tenant_local_index.astype(jnp.bfloat16)[:, None]
        which_buf = (
            jnp.zeros((owners * capacity, width_steps), jnp.bfloat16)
            .at[slot_index]
            .set(which_tenant)
            .reshape(owners, capacity, width_steps)
        )
        x_buf = lax.all_to_all(
            place(fresh_hidden_state), "batch", split_axis=0, concat_axis=0, tiled=True
        )
        query_holder = lax.all_to_all(
            place(base_query_rows), "batch", split_axis=0, concat_axis=0, tiled=True
        )
        w_buf = lax.all_to_all(which_buf, "batch", split_axis=0, concat_axis=0, tiled=True)
        lead_shape = x_buf.shape[:3]
        item_count = lead_shape[2]
        row_total_count = lead_shape[0] * lead_shape[1] * item_count
        tenant_rows = w_buf.reshape(row_total_count).astype(jnp.float32)
        select = tenant_rows[:, None] == tenant_ids[None, :]
        projected = lax.dot_general(
            x_buf.reshape(row_total_count, local_width_span),
            down_panels_every,
            (((1,), (1,)), ((), ())),
            preferred_element_type=jnp.float32,
        )
        rank_projection = jnp.sum(
            projected.reshape(row_total_count, tenant_list, rank_weight_width)
            * select[:, :, None].astype(jnp.float32),
            axis=1,
        )
        rank_projection = lax.psum(rank_projection, "tensor").astype(jnp.bfloat16)
        spread_factor = (
            select[:, :, None].astype(jnp.bfloat16) * rank_projection[:, None, :]
        ).reshape(row_total_count, tenant_list * rank_weight_width)
        adapter_query_delta = jnp.dot(
            spread_factor, up_panels_every, preferred_element_type=jnp.float32
        )
        query_rows_list = (
            query_holder.reshape(row_total_count, head_column_span).astype(jnp.float32)
            + adapter_query_delta
        ).astype(jnp.bfloat16)
        serve_mixed_out, serve_row_peak, serve_row_total = lax.map(
            attend_doc,
            (
                query_rows_list.reshape(
                    item_count, row_total_count // item_count, head_column_span
                ),
                tenant_rows.reshape(item_count, row_total_count // item_count),
            ),
        )
        q_back = query_rows_list.reshape(lead_shape + (head_column_span,))
        doc_out = serve_mixed_out.reshape(lead_shape + (head_column_span,))
        doc_peak = serve_row_peak.reshape(lead_shape + (head_count,))
        doc_total = serve_row_total.reshape(lead_shape + (head_count,))
        q_home = lax.all_to_all(q_back, "batch", split_axis=0, concat_axis=0, tiled=True)
        out_home = lax.all_to_all(doc_out, "batch", split_axis=0, concat_axis=0, tiled=True)
        peak_home = lax.all_to_all(doc_peak, "batch", split_axis=0, concat_axis=0, tiled=True)
        total_home = lax.all_to_all(doc_total, "batch", split_axis=0, concat_axis=0, tiled=True)

        def unpack(array_in):
            flat = array_in.reshape((owners * capacity,) + array_in.shape[2:])
            return jnp.take(flat, slot_index, axis=0)

        q_mine = unpack(q_home)
        out_mine = unpack(out_home)
        peak_mine = unpack(peak_home)
        total_mine = unpack(total_home)
        serve_query_rows_list = q_mine[:, 0]
        attend_query_head_rows = serve_query_rows_list.reshape(
            requests, kv_heads, group_size, HEAD_SIZE
        )
        key_heads = keys_all.reshape(requests, -1, kv_heads, HEAD_SIZE)
        value_heads = values_all.reshape(requests, -1, kv_heads, HEAD_SIZE)
        attend_scores = (
            jnp.einsum(
                "rkgd,rmkd->rkgm",
                attend_query_head_rows,
                key_heads,
                preferred_element_type=jnp.float32,
            )
            * score_scale
        )
        attend_is_valid = jnp.arange(keys_all.shape[1]) < ctx_len + step_from + 1
        attend_scores = jnp.where(attend_is_valid[None, None, None, :], attend_scores, -jnp.inf)
        attend_row_peak = jnp.max(attend_scores, axis=-1)
        attend_weights = jnp.exp(attend_scores - attend_row_peak[..., None]).astype(jnp.bfloat16)
        attend_row_total = jnp.sum(attend_weights, axis=-1, dtype=jnp.float32)
        attend_mixed_out = jnp.einsum(
            "rkgm,rmkd->rkgd", attend_weights, value_heads, preferred_element_type=jnp.float32
        )
        own_out = attend_mixed_out.reshape(requests, head_count, HEAD_SIZE)
        own_peak = attend_row_peak.reshape(requests, head_count)
        own_total = attend_row_total.reshape(requests, head_count)
        doc_peak_now = peak_mine[:, 0]
        joint = jnp.maximum(doc_peak_now, own_peak)
        doc_scale = jnp.exp(doc_peak_now - joint)
        own_scale = jnp.exp(own_peak - joint)
        numer = (
            out_mine[:, 0].reshape(requests, head_count, HEAD_SIZE) * doc_scale[..., None]
            + own_out * own_scale[..., None]
        )
        denom = total_mine[:, 0] * doc_scale + own_total * own_scale
        produced = [
            (numer / denom[..., None]).reshape(requests, head_column_span).astype(jnp.bfloat16)
        ]
        outputs = outputs + produced
    return jnp.stack(outputs, axis=1)


def solution(mesh):
    placed = (
        P("batch", None, "tensor"),
        P("batch", None, "tensor"),
        P("batch", None, "tensor"),
        P("batch", None, "tensor"),
        P("batch", None, "tensor"),
        P("batch", None, "tensor"),
        P("batch", None, "tensor"),
        P("batch", None, "tensor"),
        P("batch", None, "tensor"),
        P("batch", None, "tensor"),
        P("batch", None),
        P("batch"),
        P("batch"),
    )
    return jax.shard_map(
        local, mesh=mesh, in_specs=placed, out_specs=P("batch", None, "tensor"), check_vma=False
    )
```

profile of v0, /device:TPU:0, one launch (start us, length us, event | category | flops | bytes accessed | tf_op | source)
XLA Modules:
  0.0 270.5 jit_solution(4072282892142355669)
XLA Ops:
  3.7 7.3 %all-to-all-start = ((bf16[8,8,1]{1,2,0:T(2,128)(2,1)}), bf16[8,8,1]{1,2,0:T(2,128)(2,1)S(1)}, u32[]{:S(2)}, u32[]{:S(2)}) async-start(bf16[8,8,1]{1,2,0:T(2,128)(2,1)} %reshape.1113), calls=%async_computation | async-start | bytes 8192 | tf_op jit(solution)/shard_map/all_to_all | solution.py:106
  12.8 4.6 %all-to-all-done = bf16[8,8,1]{1,2,0:T(2,128)(2,1)S(1)} async-done(((bf16[8,8,1]{1,2,0:T(2,128)(2,1)}), bf16[8,8,1]{1,2,0:T(2,128)(2,1)S(1)}, u32[]{:S(2)}, u32[]{:S(2)}) %all-to-all-start) | async-done | bytes 160 | tf_op jit(solution)/shard_map/all_to_all | solution.py:106
  17.4 3.4 %all-to-all-start.14 = ((bf16[8,8,1,2048]{3,1,2,0:T(8,128)(2,1)}), bf16[8,8,1,2048]{3,1,2,0:T(8,128)(2,1)S(1)}, u32[]{:S(2)}, u32[]{:S(2)}) async-start(bf16[8,8,1,2048]{3,1,2,0:T(8,128)(2,1)} %bitcast.71), calls=%async_computation.14 | async-start | bytes 524288 | tf_op jit(solution)/shard_map/all_to_all | solution.py:100
  25.4 3.6 %all-to-all-done.14 = bf16[8,8,1,2048]{3,1,2,0:T(8,128)(2,1)S(1)} async-done(((bf16[8,8,1,2048]{3,1,2,0:T(8,128)(2,1)}), bf16[8,8,1,2048]{3,1,2,0:T(8,128)(2,1)S(1)}, u32[]{:S(2)}, u32[]{:S(2)}) %all-to-all-start.14) | async-done | bytes 262176 | tf_op jit(solution)/shard_map/all_to_all | solution.py:100
  29.0 3.4 %all-to-all-start.13 = ((bf16[8,8,1,2048]{3,1,2,0:T(8,128)(2,1)}), bf16[8,8,1,2048]{3,1,2,0:T(8,128)(2,1)S(1)}, u32[]{:S(2)}, u32[]{:S(2)}) async-start(bf16[8,8,1,2048]{3,1,2,0:T(8,128)(2,1)} %bitcast.68), calls=%async_computation.13 | async-start | bytes 524288 | tf_op jit(solution)/shard_map/all_to_all | solution.py:103
  35.0 5.6 %all-to-all-done.13 = bf16[8,8,1,2048]{3,1,2,0:T(8,128)(2,1)S(1)} async-done(((bf16[8,8,1,2048]{3,1,2,0:T(8,128)(2,1)}), bf16[8,8,1,2048]{3,1,2,0:T(8,128)(2,1)S(1)}, u32[]{:S(2)}, u32[]{:S(2)}) %all-to-all-start.13) | async-done | bytes 262176 | tf_op jit(solution)/shard_map/all_to_all | solution.py:103
  40.6 3.4 %all-to-all-start.8 = ((bf16[8,8,1,2048]{3,1,2,0:T(8,128)(2,1)}), bf16[8,8,1,2048]{3,1,2,0:T(8,128)(2,1)S(1)}, u32[]{:S(2)}, u32[]{:S(2)}) async-start(bf16[8,8,1,2048]{3,1,2,0:T(8,128)(2,1)} %bitcast.40), calls=%async_computation.8 | async-start | bytes 524288 | tf_op jit(solution)/shard_map/all_to_all | solution.py:100
  54.4 5.9 %all-to-all-start.2 = ((bf16[8,8,1,2048]{3,1,2,0:T(8,128)(2,1)}), bf16[8,8,1,2048]{3,1,2,0:T(8,128)(2,1)S(1)}, u32[]{:S(2)}, u32[]{:S(2)}) async-start(bf16[8,8,1,2048]{3,1,2,0:T(8,128)(2,1)} %bitcast.9), calls=%async_computation.2 | async-start | bytes 524288 | tf_op jit(solution)/shard_map/all_to_all | solution.py:100
  62.5 6.0 %all-to-all-done.2 = bf16[8,8,1,2048]{3,1,2,0:T(8,128)(2,1)S(1)} async-done(((bf16[8,8,1,2048]{3,1,2,0:T(8,128)(2,1)}), bf16[8,8,1,2048]{3,1,2,0:T(8,128)(2,1)S(1)}, u32[]{:S(2)}, u32[]{:S(2)}) %all-to-all-start.2) | async-done | bytes 262176 | tf_op jit(solution)/shard_map/all_to_all | solution.py:100
  68.6 4.0 %all-to-all-start.1 = ((bf16[8,8,1,2048]{3,1,2,0:T(8,128)(2,1)}), bf16[8,8,1,2048]{3,1,2,0:T(8,128)(2,1)}, u32[]{:S(2)}, u32[]{:S(2)}) async-start(bf16[8,8,1,2048]{3,1,2,0:T(8,128)(2,1)} %bitcast.6), calls=%async_computation.1 | async-start | bytes 524288 | tf_op jit(solution)/shard_map/all_to_all | solution.py:103
  74.4 11.5 %all-reduce = (bf16[64,64]{1,0:T(8,128)(2,1)S(1)}, bf16[64,64]{1,0:T(8,128)(2,1)S(1)}, bf16[64,64]{1,0:T(8,128)(2,1)S(1)}) all-reduce(f32[64,64]{1,0:T(8,128)} %fusion.17, f32[64,64]{1,0:T(8,128)S(1)} %fusion.15, f32[64,64]{1,0:T(8,128)S(1)} %fusion.16), channel_id=1, replica_groups=mesh['batch'=8,'tensor'=4] {'tensor'}, use_global_device_ids=true, to_apply=%region_21.25 | all-reduce | flops 12288 | bytes 73728 | tf_op jit(solution)/shard_map/psum | solution.py:123
  85.8 5.5 %all-to-all-start.7 = ((bf16[8,8,1,2048]{3,1,2,0:T(8,128)(2,1)}), bf16[8,8,1,2048]{3,1,2,0:T(8,128)(2,1)S(1)}, u32[]{:S(2)}, u32[]{:S(2)}) async-start(bf16[8,8,1,2048]{3,1,2,0:T(8,128)(2,1)} %bitcast.37), calls=%async_computation.7 | async-start | bytes 524288 | tf_op jit(solution)/shard_map/all_to_all | solution.py:103
  96.4 4.7 %all-to-all-done.7 = bf16[8,8,1,2048]{3,1,2,0:T(8,128)(2,1)S(1)} async-done(((bf16[8,8,1,2048]{3,1,2,0:T(8,128)(2,1)}), bf16[8,8,1,2048]{3,1,2,0:T(8,128)(2,1)S(1)}, u32[]{:S(2)}, u32[]{:S(2)}) %all-to-all-start.7) | async-done | bytes 262176 | tf_op jit(solution)/shard_map/all_to_all | solution.py:103
  104.6 3.8 %bitcast_reduce_fusion.2 = (f32[64,2,8]{2,0,1:T(8,128)S(1)}, f32[64,2,8]{2,0,1:T(8,128)S(1)}, f32[64,2,8]{2,0,1:T(8,128)S(1)}, f32[2,64,8,1024]{3,2,1,0:T(8,128)}) fusion(pred[64,1024]{1,0:T(8,128)(4,1)S(1)} %copy-done.7, f32[2,64,8,1024]{3,2,1,0:T(8,128)S(1)} %fusion.32, f32[2,64,8,1024]{3,2,1,0:T(8,128)S(1)} %fusion.30, ...), kind=kOutput, calls=%fused_computation.28 | convolution fusion | flops 277869568 | bytes 13447168 | tf_op jit(solution)/shard_map/while/body/eval_jaxpr/nkgd,mkd->nkgm/dot_general | solution.py:62
  109.2 3.6 %all-to-all-start.4 = ((f32[8,1,128]{2,1,0:T(1,128)}), f32[8,1,128]{2,1,0:T(1,128)S(1)}, u32[]{:S(2)}, u32[]{:S(2)}) async-start(f32[8,1,128]{2,1,0:T(1,128)} %reshape.1151), calls=%async_computation.4 | async-start | bytes 8192 | tf_op jit(solution)/shard_map/all_to_all | solution.py:149
  115.0 4.3 %all-to-all-done.4 = f32[8,1,128]{2,1,0:T(1,128)S(1)} async-done(((f32[8,1,128]{2,1,0:T(1,128)}), f32[8,1,128]{2,1,0:T(1,128)S(1)}, u32[]{:S(2)}, u32[]{:S(2)}) %all-to-all-start.4) | async-done | bytes 4128 | tf_op jit(solution)/shard_map/all_to_all | solution.py:149
  123.5 5.5 %all-to-all-done.10 = f32[8,1,128]{2,1,0:T(1,128)S(1)} async-done(((f32[8,1,128]{2,1,0:T(1,128)}), f32[8,1,128]{2,1,0:T(1,128)S(1)}, u32[]{:S(2)}, u32[]{:S(2)}) %all-to-all-start.10) | async-done | bytes 4128 | tf_op jit(solution)/shard_map/all_to_all | solution.py:149
  132.3 6.5 %convert_reduce_fusion.2 = (f32[64,2,8]{2,0,1:T(8,128)S(1)}, f32[64,2,8]{2,0,1:T(8,128)S(1)}, f32[64,2,8]{2,0,1:T(8,128)S(1)}) fusion(f32[64,2,8]{2,0,1:T(8,128)} %copy-done.8, f32[2,64,8,1024]{3,2,1,0:T(8,128)} %get-tuple-element.146, pred[64,1024]{1,0:T(8,128)(4,1)S(1)} %copy-done.7, f32[64,2,8]{2,0,1:T(8,128)S(1)} %get-tuple-element.103, ...), kind=kLoop, calls=%fused_computation.35 | loop fusion | flops 18871296 | bytes 12673024 | tf_op jit(solution)/shard_map/while/body/eval_jaxpr/reduce_sum | solution.py:69
  139.7 5.9 %all-to-all-start.6 = ((f32[8,1,128]{2,1,0:T(1,128)}), f32[8,1,128]{2,1,0:T(1,128)S(1)}, u32[]{:S(2)}, u32[]{:S(2)}) async-start(f32[8,1,128]{2,1,0:T(1,128)} %reshape.1153), calls=%async_computation.6 | async-start | bytes 8192 | tf_op jit(solution)/shard_map/all_to_all | solution.py:150
  147.0 5.0 %all-to-all-done.6 = f32[8,1,128]{2,1,0:T(1,128)S(1)} async-done(((f32[8,1,128]{2,1,0:T(1,128)}), f32[8,1,128]{2,1,0:T(1,128)S(1)}, u32[]{:S(2)}, u32[]{:S(2)}) %all-to-all-start.6) | async-done | bytes 4128 | tf_op jit(solution)/shard_map/all_to_all | solution.py:150
  156.8 5.0 %all-to-all-done.18 = f32[8,1,128]{2,1,0:T(1,128)S(1)} async-done(((f32[8,1,128]{2,1,0:T(1,128)}), f32[8,1,128]{2,1,0:T(1,128)S(1)}, u32[]{:S(2)}, u32[]{:S(2)}) %all-to-all-start.18) | async-done | bytes 4128 | tf_op jit(solution)/shard_map/all_to_all | solution.py:150
  171.5 3.7 %all-to-all-start.17 = ((bf16[8,8,1,2048]{3,1,2,0:T(8,128)(2,1)}), bf16[8,8,1,2048]{3,1,2,0:T(8,128)(2,1)S(1)}, u32[]{:S(2)}, u32[]{:S(2)}) async-start(bf16[8,8,1,2048]{3,1,2,0:T(8,128)(2,1)} %bitcast.367), calls=%async_computation.17 | async-start | bytes 524288 | tf_op jit(solution)/shard_map/all_to_all | solution.py:147
  175.2 3.6 %convolution_bitcast_fusion.5 = f32[64,2,8,128]{3,2,0,1:T(8,128)S(1)} fusion(bf16[1024,2,128,1]{2,1,0,3:T(2,128)(2,1)} %bitcast.374, f32[2,64,8,1024]{3,2,1,0:T(8,128)} %get-tuple-element.146, f32[64,2,8]{2,0,1:T(8,128)} %copy-done.8, pred[64,1024]{1,0:T(8,128)(4,1)S(1)} %copy-done.7), kind=kOutput, calls=%fused_computation.48 | convolution fusion | flops 272629760 | bytes 5312512 | tf_op jit(solution)/shard_map/while/body/eval_jaxpr/nkgm,mkd->nkgd/dot_general | solution.py:70
  179.7 3.4 %convolution_bitcast_fusion.3 = f32[64,2,8,128]{3,2,0,1:T(8,128)S(1)} fusion(bf16[1024,2,128,1]{2,1,0,3:T(2,128)(2,1)S(1)} %bitcast.375, f32[2,64,8,1024]{3,2,1,0:T(8,128)} %copy-done.2, f32[64,2,8]{2,0,1:T(8,128)S(1)} %get-tuple-element.103, pred[64,1024]{1,0:T(8,128)(4,1)S(1)} %copy-done.7), kind=kOutput, calls=%fused_computation.46 | convolution fusion | flops 272629760 | bytes 5312512 | tf_op jit(solution)/shard_map/while/body/eval_jaxpr/nkgm,mkd->nkgd/dot_general | solution.py:70
  184.1 6.0 %all-to-all-start.11 = ((bf16[8,8,1,2048]{3,1,2,0:T(8,128)(2,1)}), bf16[8,8,1,2048]{3,1,2,0:T(8,128)(2,1)S(1)}, u32[]{:S(2)}, u32[]{:S(2)}) async-start(bf16[8,8,1,2048]{3,1,2,0:T(8,128)(2,1)} %bitcast.57), calls=%async_computation.11 | async-start | bytes 524288 | tf_op jit(solution)/shard_map/all_to_all | solution.py:147
  190.1 3.4 %convolution_bitcast_fusion.4 = f32[64,2,8,128]{3,2,0,1:T(8,128)S(1)} fusion(bf16[1024,2,128,1]{2,1,0,3:T(2,128)(2,1)S(1)} %bitcast.376, f32[2,64,8,1024]{3,2,1,0:T(8,128)} %copy-done.1, f32[64,2,8]{2,0,1:T(8,128)S(1)} %get-tuple-element.102, pred[64,1024]{1,0:T(8,128)(4,1)S(1)} %copy-done.7), kind=kOutput, calls=%fused_computation.47 | convolution fusion | flops 272629760 | bytes 5312512 | tf_op jit(solution)/shard_map/while/body/eval_jaxpr/nkgm,mkd->nkgd/dot_general | solution.py:70
  198.3 4.2 %all-to-all-start.5 = ((bf16[8,8,1,2048]{3,1,2,0:T(8,128)(2,1)}), bf16[8,8,1,2048]{3,1,2,0:T(8,128)(2,1)S(1)}, u32[]{:S(2)}, u32[]{:S(2)}) async-start(bf16[8,8,1,2048]{3,1,2,0:T(8,128)(2,1)} %bitcast.26), calls=%async_computation.5 | async-start | bytes 524288 | tf_op jit(solution)/shard_map/all_to_all | solution.py:147
  204.7 6.0 %all-to-all-done.5 = bf16[8,8,1,2048]{3,1,2,0:T(8,128)(2,1)S(1)} async-done(((bf16[8,8,1,2048]{3,1,2,0:T(8,128)(2,1)}), bf16[8,8,1,2048]{3,1,2,0:T(8,128)(2,1)S(1)}, u32[]{:S(2)}, u32[]{:S(2)}) %all-to-all-start.5) | async-done | bytes 262176 | tf_op jit(solution)/shard_map/all_to_all | solution.py:147
  210.8 4.7 %all-to-all-start.9 = ((f32[8,8,1,2048]{3,1,2,0:T(8,128)}), f32[8,8,1,2048]{3,1,2,0:T(8,128)S(1)}, u32[]{:S(2)}, u32[]{:S(2)}) async-start(f32[8,8,1,2048]{3,1,2,0:T(8,128)} %bitcast.48), calls=%async_computation.9 | async-start | bytes 1048576 | tf_op jit(solution)/shard_map/all_to_all | solution.py:148
  227.7 6.0 %all-to-all-start.15 = ((f32[8,8,1,2048]{3,1,2,0:T(8,128)}), f32[8,8,1,2048]{3,1,2,0:T(8,128)S(1)}, u32[]{:S(2)}, u32[]{:S(2)}) async-start(f32[8,8,1,2048]{3,1,2,0:T(8,128)} %bitcast.79), calls=%async_computation.15 | async-start | bytes 1048576 | tf_op jit(solution)/shard_map/all_to_all | solution.py:148
  240.1 7.9 %all-to-all-done.15 = f32[8,8,1,2048]{3,1,2,0:T(8,128)S(1)} async-done(((f32[8,8,1,2048]{3,1,2,0:T(8,128)}), f32[8,8,1,2048]{3,1,2,0:T(8,128)S(1)}, u32[]{:S(2)}, u32[]{:S(2)}) %all-to-all-start.15) | async-done | bytes 524320 | tf_op jit(solution)/shard_map/all_to_all | solution.py:148
  248.0 5.1 %all-to-all-start.3 = ((f32[8,8,1,2048]{3,1,2,0:T(8,128)}), f32[8,8,1,2048]{3,1,2,0:T(8,128)S(1)}, u32[]{:S(2)}, u32[]{:S(2)}) async-start(f32[8,8,1,2048]{3,1,2,0:T(8,128)} %bitcast.17), calls=%async_computation.3 | async-start | bytes 1048576 | tf_op jit(solution)/shard_map/all_to_all | solution.py:148
  (216 shorter events, 107.2 us)
Async XLA Ops:
  0.0 91.4 %copy-start = (bf16[2,64,2048]{2,1,0:T(8,128)(2,1)S(1)}, bf16[2,64,2048]{2,1,0:T(8,128)(2,1)}, u32[]{:S(2)}) copy-start(bf16[2,64,2048]{2,1,0:T(8,128)(2,1)} %param.30) | copy-start | bytes 1572868
  0.0 52.6 %copy-start.24 = (pred[1024]{0:T(1024)(128)(4,1)S(1)}, pred[1024]{0:T(1024)(128)(4,1)}, u32[]{:S(2)}) copy-start(pred[1024]{0:T(1024)(128)(4,1)} %constant.242) | copy-start | bytes 3076
  0.0 52.0 %copy-start.27 = (s32[32,1]{0,1:T(1,128)S(1)}, s32[32,1]{0,1:T(1,128)}, u32[]{:S(2)}) copy-start(s32[32,1]{0,1:T(1,128)} %param.31) | copy-start | bytes 388
  0.0 50.1 %copy-start.17 = (bf16[32,3,256]{2,0,1:T(8,128)(2,1)S(1)}, bf16[32,3,256]{2,0,1:T(8,128)(2,1)}, u32[]{:S(2)}) copy-start(bf16[32,3,256]{2,0,1:T(8,128)(2,1)} %param.23) | copy-start | bytes 147460
  3.7 13.7 %all-to-all-start = ((bf16[8,8,1]{1,2,0:T(2,128)(2,1)}), bf16[8,8,1]{1,2,0:T(2,128)(2,1)S(1)}, u32[]{:S(2)}, u32[]{:S(2)}) async-start(bf16[8,8,1]{1,2,0:T(2,128)(2,1)} %reshape.1113), calls=%async_computation | async-start | bytes 8192 | tf_op jit(solution)/shard_map/all_to_all | solution.py:106
  12.8 59.8 %copy-start.3 = (bf16[2,64,2048]{2,1,0:T(8,128)(2,1)S(1)}, bf16[2,64,2048]{2,1,0:T(8,128)(2,1)}, u32[]{:S(2)}) copy-start(bf16[2,64,2048]{2,1,0:T(8,128)(2,1)} %param.29) | copy-start | bytes 1572868
  17.4 11.6 %all-to-all-start.14 = ((bf16[8,8,1,2048]{3,1,2,0:T(8,128)(2,1)}), bf16[8,8,1,2048]{3,1,2,0:T(8,128)(2,1)S(1)}, u32[]{:S(2)}, u32[]{:S(2)}) async-start(bf16[8,8,1,2048]{3,1,2,0:T(8,128)(2,1)} %bitcast.71), calls=%async_computation.14 | async-start | bytes 524288 | tf_op jit(solution)/shard_map/all_to_all | solution.py:100
  29.0 11.6 %all-to-all-start.13 = ((bf16[8,8,1,2048]{3,1,2,0:T(8,128)(2,1)}), bf16[8,8,1,2048]{3,1,2,0:T(8,128)(2,1)S(1)}, u32[]{:S(2)}, u32[]{:S(2)}) async-start(bf16[8,8,1,2048]{3,1,2,0:T(8,128)(2,1)} %bitcast.68), calls=%async_computation.13 | async-start | bytes 524288 | tf_op jit(solution)/shard_map/all_to_all | solution.py:103
  40.6 13.8 %all-to-all-start.8 = ((bf16[8,8,1,2048]{3,1,2,0:T(8,128)(2,1)}), bf16[8,8,1,2048]{3,1,2,0:T(8,128)(2,1)S(1)}, u32[]{:S(2)}, u32[]{:S(2)}) async-start(bf16[8,8,1,2048]{3,1,2,0:T(8,128)(2,1)} %bitcast.40), calls=%async_computation.8 | async-start | bytes 524288 | tf_op jit(solution)/shard_map/all_to_all | solution.py:100
  54.4 14.2 %all-to-all-start.2 = ((bf16[8,8,1,2048]{3,1,2,0:T(8,128)(2,1)}), bf16[8,8,1,2048]{3,1,2,0:T(8,128)(2,1)S(1)}, u32[]{:S(2)}, u32[]{:S(2)}) async-start(bf16[8,8,1,2048]{3,1,2,0:T(8,128)(2,1)} %bitcast.9), calls=%async_computation.2 | async-start | bytes 524288 | tf_op jit(solution)/shard_map/all_to_all | solution.py:100
  68.6 17.3 %all-to-all-start.1 = ((bf16[8,8,1,2048]{3,1,2,0:T(8,128)(2,1)}), bf16[8,8,1,2048]{3,1,2,0:T(8,128)(2,1)}, u32[]{:S(2)}, u32[]{:S(2)}) async-start(bf16[8,8,1,2048]{3,1,2,0:T(8,128)(2,1)} %bitcast.6), calls=%async_computation.1 | async-start | bytes 524288 | tf_op jit(solution)/shard_map/all_to_all | solution.py:103
  85.8 15.2 %all-to-all-start.7 = ((bf16[8,8,1,2048]{3,1,2,0:T(8,128)(2,1)}), bf16[8,8,1,2048]{3,1,2,0:T(8,128)(2,1)S(1)}, u32[]{:S(2)}, u32[]{:S(2)}) async-start(bf16[8,8,1,2048]{3,1,2,0:T(8,128)(2,1)} %bitcast.37), calls=%async_computation.7 | async-start | bytes 524288 | tf_op jit(solution)/shard_map/all_to_all | solution.py:103
  104.6 18.0 %copy-start.23 = (s32[32]{0:T(128)S(1)}, s32[32]{0:T(128)}, u32[]{:S(2)}) copy-start(s32[32]{0:T(128)} %get-tuple-element.129) | copy-start | bytes 388
  109.2 10.1 %all-to-all-start.4 = ((f32[8,1,128]{2,1,0:T(1,128)}), f32[8,1,128]{2,1,0:T(1,128)S(1)}, u32[]{:S(2)}, u32[]{:S(2)}) async-start(f32[8,1,128]{2,1,0:T(1,128)} %reshape.1151), calls=%async_computation.4 | async-start | bytes 8192 | tf_op jit(solution)/shard_map/all_to_all | solution.py:149
  119.3 9.7 %all-to-all-start.10 = ((f32[8,1,128]{2,1,0:T(1,128)}), f32[8,1,128]{2,1,0:T(1,128)S(1)}, u32[]{:S(2)}, u32[]{:S(2)}) async-start(f32[8,1,128]{2,1,0:T(1,128)} %reshape.1147), calls=%async_computation.10 | async-start | bytes 8192 | tf_op jit(solution)/shard_map/all_to_all | solution.py:149
  122.6 92.8 %copy-start.18 = (s32[1024]{0:T(1024)}, s32[1024]{0:T(1024)S(1)}, u32[]{:S(2)}) copy-start(s32[1024]{0:T(1024)S(1)} %pad_clamp_fusion) | copy-start | bytes 12292
  129.0 10.7 %all-to-all-start.16 = ((f32[8,1,128]{2,1,0:T(1,128)}), f32[8,1,128]{2,1,0:T(1,128)S(1)}, u32[]{:S(2)}, u32[]{:S(2)}) async-start(f32[8,1,128]{2,1,0:T(1,128)} %reshape.1143), calls=%async_computation.16 | async-start | bytes 8192 | tf_op jit(solution)/shard_map/all_to_all | solution.py:149
  139.7 12.4 %all-to-all-start.6 = ((f32[8,1,128]{2,1,0:T(1,128)}), f32[8,1,128]{2,1,0:T(1,128)S(1)}, u32[]{:S(2)}, u32[]{:S(2)}) async-start(f32[8,1,128]{2,1,0:T(1,128)} %reshape.1153), calls=%async_computation.6 | async-start | bytes 8192 | tf_op jit(solution)/shard_map/all_to_all | solution.py:150
  152.1 9.7 %all-to-all-start.18 = ((f32[8,1,128]{2,1,0:T(1,128)}), f32[8,1,128]{2,1,0:T(1,128)S(1)}, u32[]{:S(2)}, u32[]{:S(2)}) async-start(f32[8,1,128]{2,1,0:T(1,128)} %reshape.1145), calls=%async_computation.18 | async-start | bytes 8192 | tf_op jit(solution)/shard_map/all_to_all | solution.py:150
  161.8 9.7 %all-to-all-start.12 = ((f32[8,1,128]{2,1,0:T(1,128)}), f32[8,1,128]{2,1,0:T(1,128)S(1)}, u32[]{:S(2)}, u32[]{:S(2)}) async-start(f32[8,1,128]{2,1,0:T(1,128)} %reshape.1149), calls=%async_computation.12 | async-start | bytes 8192 | tf_op jit(solution)/shard_map/all_to_all | solution.py:150
  171.5 12.7 %all-to-all-start.17 = ((bf16[8,8,1,2048]{3,1,2,0:T(8,128)(2,1)}), bf16[8,8,1,2048]{3,1,2,0:T(8,128)(2,1)S(1)}, u32[]{:S(2)}, u32[]{:S(2)}) async-start(bf16[8,8,1,2048]{3,1,2,0:T(8,128)(2,1)} %bitcast.367), calls=%async_computation.17 | async-start | bytes 524288 | tf_op jit(solution)/shard_map/all_to_all | solution.py:147
  184.1 14.2 %all-to-all-start.11 = ((bf16[8,8,1,2048]{3,1,2,0:T(8,128)(2,1)}), bf16[8,8,1,2048]{3,1,2,0:T(8,128)(2,1)S(1)}, u32[]{:S(2)}, u32[]{:S(2)}) async-start(bf16[8,8,1,2048]{3,1,2,0:T(8,128)(2,1)} %bitcast.57), calls=%async_computation.11 | async-start | bytes 524288 | tf_op jit(solution)/shard_map/all_to_all | solution.py:147
  193.5 27.1 %copy-start.20 = (f32[8,1,128]{2,1,0:T(1,128)S(1)}, f32[8,1,128]{2,1,0:T(1,128)}, u32[]{:S(2)}) copy-start(f32[8,1,128]{2,1,0:T(1,128)} %copy-done.19) | copy-start | bytes 12292
  193.5 31.4 %copy-start.21 = (pred[32]{0:T(512)(128)(4,1)S(1)}, pred[32]{0:T(512)(128)(4,1)}, u32[]{:S(2)}) copy-start(pred[32]{0:T(512)(128)(4,1)} %get-tuple-element.128) | copy-start | bytes 100
  194.4 31.3 %copy-start.26 = (pred[67]{0:T(512)(128)(4,1)S(1)}, pred[67]{0:T(512)(128)(4,1)}, u32[]{:S(2)}) copy-start(pred[67]{0:T(512)(128)(4,1)} %iota_compare_fusion.2) | copy-start | bytes 205
  198.3 12.4 %all-to-all-start.5 = ((bf16[8,8,1,2048]{3,1,2,0:T(8,128)(2,1)}), bf16[8,8,1,2048]{3,1,2,0:T(8,128)(2,1)S(1)}, u32[]{:S(2)}, u32[]{:S(2)}) async-start(bf16[8,8,1,2048]{3,1,2,0:T(8,128)(2,1)} %bitcast.26), calls=%async_computation.5 | async-start | bytes 524288 | tf_op jit(solution)/shard_map/all_to_all | solution.py:147
  210.8 17.0 %all-to-all-start.9 = ((f32[8,8,1,2048]{3,1,2,0:T(8,128)}), f32[8,8,1,2048]{3,1,2,0:T(8,128)S(1)}, u32[]{:S(2)}, u32[]{:S(2)}) async-start(f32[8,8,1,2048]{3,1,2,0:T(8,128)} %bitcast.48), calls=%async_computation.9 | async-start | bytes 1048576 | tf_op jit(solution)/shard_map/all_to_all | solution.py:148
  227.7 20.3 %all-to-all-start.15 = ((f32[8,8,1,2048]{3,1,2,0:T(8,128)}), f32[8,8,1,2048]{3,1,2,0:T(8,128)S(1)}, u32[]{:S(2)}, u32[]{:S(2)}) async-start(f32[8,8,1,2048]{3,1,2,0:T(8,128)} %bitcast.79), calls=%async_computation.15 | async-start | bytes 1048576 | tf_op jit(solution)/shard_map/all_to_all | solution.py:148
  239.5 17.7 %copy-start.10 = (f32[32,16]{1,0:T(8,128)S(1)}, f32[32,16]{1,0:T(8,128)}, u32[]{:S(2)}) copy-start(f32[32,16]{1,0:T(8,128)} %gather_fusion.9) | copy-start | bytes 6148
  239.5 17.7 %copy-start.11 = (f32[32,16]{1,0:T(8,128)S(1)}, f32[32,16]{1,0:T(8,128)}, u32[]{:S(2)}) copy-start(f32[32,16]{1,0:T(8,128)} %gather_fusion.3) | copy-start | bytes 6148
  239.5 17.7 %copy-start.12 = (f32[32,16]{1,0:T(8,128)S(1)}, f32[32,16]{1,0:T(8,128)}, u32[]{:S(2)}) copy-start(f32[32,16]{1,0:T(8,128)} %gather_fusion.11) | copy-start | bytes 6148
  248.0 19.0 %all-to-all-start.3 = ((f32[8,8,1,2048]{3,1,2,0:T(8,128)}), f32[8,8,1,2048]{3,1,2,0:T(8,128)S(1)}, u32[]{:S(2)}, u32[]{:S(2)}) async-start(f32[8,8,1,2048]{3,1,2,0:T(8,128)} %bitcast.17), calls=%async_computation.3 | async-start | bytes 1048576 | tf_op jit(solution)/shard_map/all_to_all | solution.py:148
  (15 other events, 135.1 us)
where the time goes:
time: 273 us; the launch traced here: 270 us
  starting transfers between devices  85.3 us (31%)
  waiting for transfers between devices  62.4 us (23%)
  local copies, waits for them, and re-layouts  53.9 us (20%)
  matrix products  30.2 us (11%)
  other arithmetic  26.4 us (10%)
  blocking collectives  11.5 us (4%)
    all_to_all x3, starting transfers between devices, local(): lax.all_to_all(doc_out, 'batch', split_axis=0, concat_axis=0, tiled=True)  15.8 us
    all_to_all x3, starting transfers between devices, local(): lax.all_to_all(q_back, 'batch', split_axis=0, concat_axis=0, tiled=True)  13.8 us
    all_to_all x3, starting transfers between devices, local(): lax.all_to_all(place(base_query_rows), 'batch', split_axis=0, concat_axis...  13 us
    all_to_all x3, starting transfers between devices, local(): lax.all_to_all(place(fresh_hidden_state), 'batch', split_axis=0, concat_a...  12.8 us
    all_to_all x3, starting transfers between devices, local(): lax.all_to_all(doc_total, 'batch', split_axis=0, concat_axis=0, tiled=True)  12.5 us
    all_to_all x3, waiting for transfers between devices, local(): lax.all_to_all(doc_total, 'batch', split_axis=0, concat_axis=0, tiled=True)  12.3 us
    psum x1, blocking collectives, local(): rank_projection = lax.psum(rank_projection, 'tensor').astype(jnp.bfloat16)  11.5 us
    gather x12, local copies, waits for them, and re-layouts, unpack(): return jnp.take(flat, slot_index, axis=0)  11.2 us
  transfers between devices with their start and end apart: 19, of which 13 were waited for; matrix products, arithmetic and copies ran while one was open for 35% of the time, Pallas kernels for 0%

commit v1 on v0

v1 whole, which is shorter than its diff:
```python
import functools

import jax
import jax.numpy as jnp
from jax import lax
from jax.experimental import pallas as pl
from jax.experimental.pallas import tpu as pltpu
from jax.sharding import PartitionSpec as P

HEAD = 128
DOC_BLOCK = 128
LOG2E = 1.4426950408889634
LOW = -1e30
GROUP = 8
MESH = pl.DeviceIdType.MESH
F32 = jnp.float32
BF16 = jnp.bfloat16


def iota(shape, axis):
    return lax.broadcasted_iota(jnp.int32, shape, axis)


def split_index(index, size, count):
    high = jnp.zeros_like(index)
    for k in range(1, count):
        high = high + (index >= k * size).astype(jnp.int32)
    return high, index - high * size


def dot(a, b):
    return jnp.dot(a, b, preferred_element_type=F32)


def dot_nt(a, b):
    return lax.dot_general(a, b, (((1,), (1,)), ((), ())), preferred_element_type=F32)


def kernel(
    n, tn, cap, rows,
    x_ref, b_ref, fk_ref, fv_ref, own_ref, loc_ref, cnt_ref,
    ck_hbm, cv_hbm, dk_hbm, dv_hbm, down_hbm, up_hbm,
    out_ref,
    ck, cv, dk, dv, down, up,
    sx, rx, sb, rb, sq, rq, so, ro, part,
    delta, bias, lse, qh, own_out, own_lse,
    in_sem, x_s, x_r, b_s, b_r, q_s, q_r, o_s, o_r, p_s, p_r,
):
    steps, reqs, width = x_ref.shape
    cols = b_ref.shape[2]
    heads = cols // HEAD
    kvs = fk_ref.shape[2] // HEAD
    per_kv = heads // kvs
    tenants, doc_len, _ = dk.shape
    rank = down.shape[1]
    ctx = ck.shape[1]
    total = n * rows
    home = steps * reqs
    half = cols // kvs
    scale = LOG2E * HEAD ** -0.5
    me = lax.axis_index("batch")
    mt = lax.axis_index("tensor")

    barrier = pltpu.get_barrier_semaphore()

    @pl.loop(1, n)
    def _(i):
        pl.semaphore_signal(barrier, inc=1, device_id={"batch": lax.rem(me + i, n)}, device_id_type=MESH)

    for i in range(1, tn):
        pl.semaphore_signal(barrier, inc=1, device_id={"tensor": lax.rem(mt + i, tn)}, device_id_type=MESH)

    loads = [
        pltpu.make_async_copy(src, dst, in_sem.at[k])
        for k, (src, dst) in enumerate(
            [(down_hbm, down), (up_hbm, up), (dk_hbm, dk), (dv_hbm, dv), (ck_hbm, ck), (cv_hbm, cv)]
        )
    ]
    for load in loads:
        load.start()

    owner_col = own_ref[...]
    wide_step, wide_req = split_index(iota((reqs, home), 1), reqs, steps)
    sub = iota((reqs, home), 0)
    owner_wide = jnp.sum(jnp.where(sub == wide_req, owner_col, 0), axis=0, keepdims=True)
    rank_wide = jnp.sum(
        jnp.where((owner_wide == owner_col) & (sub < wide_req), 1, 0), axis=0, keepdims=True
    )
    row_step, row_slot = split_index(iota((rows, home), 0), cap, steps + 1)
    row_hit = (row_step == wide_step[:1]) & (row_slot == rank_wide)
    pack = jnp.concatenate(
        [jnp.where(row_hit & (owner_wide == o), 1.0, 0.0) for o in range(n)], axis=0
    ).astype(BF16)

    tenant_tall = jnp.concatenate(
        [jnp.broadcast_to(loc_ref[...].astype(F32), (reqs, HEAD))] * steps, axis=0
    ).astype(BF16)
    x_all = x_ref[...].reshape(home, width)
    sx[:, :, width:] = dot(pack, tenant_tall).reshape(n, rows, HEAD).astype(BF16)
    for c in range(0, width, 512):
        sx[:, :, c : c + 512] = dot(pack, x_all[:, c : c + 512]).reshape(n, rows, 512).astype(BF16)

    def copy(src, dst, ssem, rsem, i):
        to = lax.rem(me + i, n)
        return pltpu.make_async_remote_copy(
            src_ref=src.at[to], dst_ref=dst.at[me], send_sem=ssem.at[i], recv_sem=rsem.at[i],
            device_id={"batch": to}, device_id_type=MESH,
        )

    def landed(src, dst, ssem, rsem, i):
        come = lax.rem(me - i + n, n)
        pltpu.make_async_remote_copy(
            src_ref=src.at[come], dst_ref=dst.at[come], send_sem=ssem.at[i], recv_sem=rsem.at[i],
            device_id={"batch": come}, device_id_type=MESH,
        ).wait_recv()
        return come

    def start_all(*refs):
        @pl.loop(1, n)
        def _(i):
            copy(*refs, i).start()

    def wait_all(*refs):
        @pl.loop(1, n)
        def _(i):
            landed(*refs, i)

    def sent_all(*refs):
        @pl.loop(1, n)
        def _(i):
            copy(*refs, i).wait_send()

    def stacked(ref, lo, size):
        return jnp.concatenate(
            [ref[j, :, lo : lo + size].astype(F32) for j in range(n)], axis=0
        )

    pl.semaphore_wait(barrier, n - 1 + tn - 1)
    start_all(sx, rx, x_s, x_r)
    rx[me] = sx[me]

    b_all = b_ref[...].reshape(home, cols)
    for c in range(0, cols, 512):
        sb[:, :, c : c + 512] = dot(pack, b_all[:, c : c + 512]).reshape(n, rows, 512).astype(BF16)
    start_all(sb, rb, b_s, b_r)
    rb[me] = sb[me]

    loads[0].wait()
    wait_all(sx, rx, x_s, x_r)
    tenant_rows = stacked(rx, width, HEAD)
    low = jnp.zeros((total, tenants * rank), F32)
    for c in range(0, width, 512):
        low = low + dot_nt(
            stacked(rx, c, 512).astype(BF16), down[:, :, c : c + 512].reshape(tenants * rank, 512)
        )
    lane_tenant, _ = split_index(iota((total, tenants * rank), 1), rank, tenants)
    part[mt] = jnp.where(lane_tenant == tenant_rows[:, :1].astype(jnp.int32), low, 0.0)

    def part_copy(i):
        to = lax.rem(mt + i, tn)
        return pltpu.make_async_remote_copy(
            src_ref=part.at[mt], dst_ref=part.at[mt], send_sem=p_s.at[i], recv_sem=p_r.at[i],
            device_id={"tensor": to}, device_id_type=MESH,
        )

    for i in range(1, tn):
        part_copy(i).start()

    key = iota((total, doc_len), 1)
    for t in range(tenants):
        sees = (tenant_rows[:, :1] == float(t)) & (key < DOC_BLOCK * cnt_ref[t])
        bias[:, t * doc_len : (t + 1) * doc_len] = jnp.where(sees, 0.0, LOW)
    lse[...] = jnp.zeros_like(lse)

    loads[1].wait()
    for i in range(1, tn):
        come = lax.rem(mt - i + tn, tn)
        pltpu.make_async_remote_copy(
            src_ref=part.at[come], dst_ref=part.at[come], send_sem=p_s.at[i], recv_sem=p_r.at[i],
            device_id={"tensor": come}, device_id_type=MESH,
        ).wait_recv()
    spread = part[0]
    for i in range(1, tn):
        spread = spread + part[i]
    spread = spread.astype(BF16)
    for c in range(0, cols, 512):
        delta[:, c : c + 512] = dot(spread, up[:, :, c : c + 512].reshape(tenants * rank, 512))

    def adapt(j):
        here = pl.ds(pl.multiple_of(j * rows, 8), rows)
        q = (rb[j].astype(F32) + delta[here, :]).astype(BF16)
        sq[j] = q
        delta[here, :] = q.astype(F32)

    adapt(me)
    rq[me] = sq[me]

    @pl.loop(1, n)
    def _(i):
        j = landed(sb, rb, b_s, b_r, i)
        adapt(j)
        pltpu.make_async_remote_copy(
            src_ref=sq.at[j], dst_ref=rq.at[me], send_sem=q_s.at[n - i], recv_sem=q_r.at[n - i],
            device_id={"batch": j}, device_id_type=MESH,
        ).start()

    loads[2].wait()
    loads[3].wait()
    lane = iota((total, HEAD), 1)
    _, lane_head = split_index(lane, heads, HEAD // heads)
    for k in range(kvs):
        mine = slice(k * HEAD, (k + 1) * HEAD)

        @pl.loop(0, per_kv)
        def _(g):
            h = k * per_kv + g
            at = pl.ds(pl.multiple_of(h * HEAD, HEAD), HEAD)
            q = delta[:, at].astype(BF16)
            keys = dk[:, :, mine].reshape(tenants * doc_len, HEAD)
            s = dot_nt(q, keys) * scale + bias[...]
            peak = jnp.max(s, axis=1, keepdims=True)
            w = jnp.exp2(s - peak).astype(BF16)
            amount = jnp.sum(w.astype(F32), axis=1, keepdims=True)
            mixed = dot(w, dv[:, :, mine].reshape(tenants * doc_len, HEAD)) / amount
            so[:, :, at] = mixed.reshape(n, rows, HEAD).astype(BF16)
            lse[...] = jnp.where(lane_head == h, peak + jnp.log2(amount), lse[...])

        if k == kvs - 1:
            value = lse[...]
            first = value.astype(BF16).astype(F32)
            second = (value - first).astype(BF16).astype(F32)
            third = value - first - second
            pieces = jnp.where(
                lane < heads, first,
                jnp.where(lane < 2 * heads, second, jnp.where(lane < 3 * heads, third, 0.0)),
            )
            so[:, :, cols:] = pieces.reshape(n, rows, HEAD).astype(BF16)
        lo, size = k * half, half + (HEAD if k == kvs - 1 else 0)
        chunk = (so.at[:, :, lo : lo + size], ro.at[:, :, lo : lo + size], o_s.at[k], o_r.at[k])
        start_all(*chunk)
        ro[me, :, lo : lo + size] = so[me, :, lo : lo + size]

    tall_step, tall_req = split_index(iota((home, total), 0), reqs, steps)
    owner_tall = jnp.concatenate([owner_col] * steps, axis=0)
    rank_col = jnp.sum(
        jnp.where((owner_col == owner_wide[:, :reqs]) & (iota((reqs, reqs), 1) < iota((reqs, reqs), 0)), 1, 0),
        axis=1, keepdims=True,
    )
    rank_tall = jnp.concatenate([rank_col] * steps, axis=0)
    slot_owner, slot_row = split_index(iota((1, total), 1), rows, n)
    unpack = jnp.where(
        (slot_owner == owner_tall) & (slot_row == tall_step * cap + rank_tall), 1.0, 0.0
    ).astype(BF16)
    wait_all(sq, rq, q_s, q_r)
    for c in range(0, cols, 512):
        qh[:, c : c + 512] = dot(unpack, stacked(rq, c, 512).astype(BF16))
    own_lse[...] = jnp.zeros_like(own_lse)
    loads[4].wait()
    loads[5].wait()
    size = per_kv * steps * GROUP
    _, inner = split_index(iota((size, 1), 0), steps * GROUP, per_kv)
    q_step, q_req = split_index(inner, GROUP, steps)
    key_req, _ = split_index(iota((1, GROUP * ctx), 1), ctx, GROUP)
    f_step, f_req = split_index(iota((1, home), 1), reqs, steps)
    ctx_bias = jnp.where(q_req == key_req, 0.0, LOW)
    for g in range(reqs // GROUP):
        fresh_bias = jnp.where((q_req + g * GROUP == f_req) & (f_step <= q_step), 0.0, LOW)
        for k in range(kvs):
            mine = slice(k * HEAD, (k + 1) * HEAD)
            places = [
                (slice(s * reqs + g * GROUP, s * reqs + (g + 1) * GROUP), h)
                for h in range(k * per_kv, (k + 1) * per_kv)
                for s in range(steps)
            ]
            q = jnp.concatenate(
                [qh[r, h * HEAD : (h + 1) * HEAD] for r, h in places], axis=0
            ).astype(BF16)
            keys = ck[g * GROUP : (g + 1) * GROUP, :, mine].reshape(GROUP * ctx, HEAD)
            values = cv[g * GROUP : (g + 1) * GROUP, :, mine].reshape(GROUP * ctx, HEAD)
            sc = dot_nt(q, keys) * scale + ctx_bias
            sf = dot_nt(q, fk_ref[:, :, mine].reshape(home, HEAD)) * scale + fresh_bias
            peak = jnp.maximum(jnp.max(sc, axis=1, keepdims=True), jnp.max(sf, axis=1, keepdims=True))
            wc = jnp.exp2(sc - peak).astype(BF16)
            wf = jnp.exp2(sf - peak).astype(BF16)
            amount = jnp.sum(wc.astype(F32), axis=1, keepdims=True) + jnp.sum(
                wf.astype(F32), axis=1, keepdims=True
            )
            mixed = (dot(wc, values) + dot(wf, fv_ref[:, :, mine].reshape(home, HEAD))) / amount
            level = peak + jnp.log2(amount)
            for e, (r, h) in enumerate(places):
                piece = slice(e * GROUP, (e + 1) * GROUP)
                own_out[r, h * HEAD : (h + 1) * HEAD] = mixed[piece]
                own_lse[r, :] = jnp.where(
                    iota((GROUP, HEAD), 1) == h, level[piece], own_lse[r, :]
                )

    for k in range(kvs):
        lo, size = k * half, half + (HEAD if k == kvs - 1 else 0)
        wait_all(so.at[:, :, lo : lo + size], ro.at[:, :, lo : lo + size], o_s.at[k], o_r.at[k])
    from_piece, from_head = split_index(iota((HEAD, HEAD), 0), heads, HEAD // heads)
    fold = jnp.where(
        (from_head == iota((HEAD, HEAD), 1)) & (from_piece < 3), 1.0, 0.0
    ).astype(BF16)
    doc_lse = dot(dot(unpack, stacked(ro, cols, HEAD).astype(BF16)).astype(BF16), fold)
    top = jnp.maximum(doc_lse, own_lse[...])
    doc_part = jnp.exp2(doc_lse - top)
    own_part = jnp.exp2(own_lse[...] - top)
    alpha = doc_part / (doc_part + own_part)
    for c in range(0, cols, 512):
        doc = dot(unpack, stacked(ro, c, 512).astype(BF16))
        for h in range(c // HEAD, (c + 512) // HEAD):
            own = own_out[:, h * HEAD : (h + 1) * HEAD]
            weight = alpha[:, h : h + 1]
            both = doc[:, h * HEAD - c : (h + 1) * HEAD - c] * weight + own * (1.0 - weight)
            out_ref[:, :, h * HEAD : (h + 1) * HEAD] = both.reshape(steps, reqs, HEAD).astype(BF16)

    sent_all(sx, rx, x_s, x_r)
    sent_all(sb, rb, b_s, b_r)
    sent_all(sq, rq, q_s, q_r)
    for k in range(kvs):
        lo, size = k * half, half + (HEAD if k == kvs - 1 else 0)
        sent_all(so.at[:, :, lo : lo + size], ro.at[:, :, lo : lo + size], o_s.at[k], o_r.at[k])
    for i in range(1, tn):
        part_copy(i).wait_send()


def local(
    fresh_hidden_state,
    base_query_rows,
    fresh_key_rows,
    fresh_value_rows,
    context_key_cache,
    context_value_cache,
    document_key_rows,
    document_value_rows,
    adapter_down_panel,
    adapter_up_panel,
    tenant_owner_batch,
    tenant_local_index,
    document_block_count,
):
    reqs, steps, width = fresh_hidden_state.shape
    cols = base_query_rows.shape[2]
    n = lax.axis_size("batch")
    tn = lax.axis_size("tensor")
    cap = max(2, 2 * reqs // n)
    rows = -(-cap * steps // 8) * 8
    kvs = fresh_key_rows.shape[2] // HEAD
    tenants, rank, _ = adapter_down_panel.shape
    doc_len = document_key_rows.shape[1]
    total = n * rows
    home = reqs * steps
    vmem = pl.BlockSpec(memory_space=pltpu.VMEM)
    smem = pl.BlockSpec(memory_space=pltpu.SMEM)
    hbm = pl.BlockSpec(memory_space=pl.ANY)
    dma = pltpu.SemaphoreType.DMA
    out = pl.pallas_call(
        functools.partial(kernel, n, tn, cap, rows),
        out_shape=jax.ShapeDtypeStruct((steps, reqs, cols), BF16),
        in_specs=[vmem] * 6 + [smem] + [hbm] * 6,
        out_specs=vmem,
        scratch_shapes=[
            pltpu.VMEM(a.shape, BF16)
            for a in (
                context_key_cache, context_value_cache, document_key_rows,
                document_value_rows, adapter_down_panel, adapter_up_panel,
            )
        ]
        + [pltpu.VMEM((n, rows, width + HEAD), BF16)] * 2
        + [pltpu.VMEM((n, rows, cols), BF16)] * 4
        + [pltpu.VMEM((n, rows, cols + HEAD), BF16)] * 2
        + [
            pltpu.VMEM((tn, total, tenants * rank), F32),
            pltpu.VMEM((total, cols), F32),
            pltpu.VMEM((total, tenants * doc_len), F32),
            pltpu.VMEM((total, HEAD), F32),
            pltpu.VMEM((home, cols), F32),
            pltpu.VMEM((home, cols), F32),
            pltpu.VMEM((home, HEAD), F32),
            dma((6,)),
        ]
        + [dma((n,))] * 6
        + [dma((kvs, n))] * 2
        + [dma((tn,))] * 2,
        compiler_params=pltpu.CompilerParams(
            collective_id=0, has_side_effects=True, vmem_limit_bytes=56 * 2**20
        ),
    )(
        fresh_hidden_state.transpose(1, 0, 2),
        base_query_rows.transpose(1, 0, 2),
        fresh_key_rows.transpose(1, 0, 2),
        fresh_value_rows.transpose(1, 0, 2),
        tenant_owner_batch,
        tenant_local_index[:, None],
        document_block_count,
        context_key_cache,
        context_value_cache,
        document_key_rows,
        document_value_rows,
        adapter_down_panel,
        adapter_up_panel,
    )
    return out.transpose(1, 0, 2)


def solution(mesh):
    cut = P("batch", None, "tensor")
    placed = (cut,) * 10 + (P("batch", None), P("batch"), P("batch"))
    return jax.shard_map(local, mesh=mesh, in_specs=placed, out_specs=cut, check_vma=False)
```

time: 273 us -> 87.7 us (0.32)
  starting transfers between devices: 85.3 us -> 0 us
  Pallas kernels: 0 us -> 83.7 us
  waiting for transfers between devices: 62.4 us -> 0 us
  local copies, waits for them, and re-layouts: 53.9 us -> 3.8 us
  matrix products: 30.2 us -> 0 us
  other arithmetic: 26.4 us -> 0 us
  blocking collectives: 11.5 us -> 0 us
    all_to_all x19 -> x0, starting transfers between devices: 85.3 us -> none  [the longest x3 15.8 us: local(): lax.all_to_all(doc_out, 'batch', split_axis=0, concat_axis=0, tiled=True)]
    pallas_call x0 -> x1, Pallas kernels: none -> 83.7 us  [local(): pl.pallas_call(functools.partial(kernel, n, tn, cap, rows), out_shape=jax...]
    all_to_all x19 -> x0, waiting for transfers between devices: 62.4 us -> none  [the longest x3 12.3 us: local(): lax.all_to_all(doc_total, 'batch', split_axis=0, concat_axis=0, tiled=True)]
    dot_general x18 -> x0, matrix products: 30.2 us -> none  [the longest x3 10.3 us: attend_doc(): jnp.einsum('nkgm,mkd->nkgd', weights, doc_v, preferred_element_type=jnp.f...]
    scatter x7 -> x0, local copies, waits for them, and re-layouts: 11.9 us -> none  [the longest x6 11.1 us: place(): return buffer.at[slot_index].set(value_rows_list[:, step_from:step_upto])...]
    gather x13 -> x0, local copies, waits for them, and re-layouts: 11.8 us -> none  [the longest x12 11.2 us: unpack(): return jnp.take(flat, slot_index, axis=0)]
    reshape x29 -> x0, local copies, waits for them, and re-layouts: 11.6 us -> none  [the longest x3 2.76 us: local(): doc_out = serve_mixed_out.reshape(lead_shape + (head_column_span,))]
    psum x1 -> x0, blocking collectives: 11.5 us -> none  [local(): rank_projection = lax.psum(rank_projection, 'tensor').astype(jnp.bfloat16)]
  transfers between devices with their start and end apart: 19 -> 0, of which waited for: 13 -> 0; matrix products, arithmetic and copies ran while one was open for 35% -> 0% of each run, Pallas kernels for 0% -> 0%
where the time goes in v1:
time: 87.7 us; the launch traced here: 87.5 us
  Pallas kernels  83.7 us (95%)
  local copies, waits for them, and re-layouts  3.8 us (4%)
    pallas_call x1, Pallas kernels, local(): pl.pallas_call(functools.partial(kernel, n, tn, cap, rows), out_shape=jax...  83.7 us
    unnamed x6, local copies, waits for them, and re-layouts  3.12 us

profile of v1, /device:TPU:0, one launch (start us, length us, event | category | flops | bytes accessed | tf_op | source)
XLA Modules:
  0.0 87.5 jit_solution(16577450365222429936)
XLA Ops:
  0.0 0.0 copy-start
  0.0 0.7 copy-done
  0.7 0.0 copy-start.1
  0.7 0.7 copy.14.own_ref
  1.3 0.0 copy-done.1
  1.4 0.7 copy.15.loc_ref
  2.0 83.7 %shard_map.127 = bf16[3,32,2048]{2,1,0:T(8,128)(2,1)} custom-call(bf16[3,32,2048]{2,1,0:T(8,128)(2,1)} %bitcast.7, bf16[3,32,2048]{2,1,0:T(8,128)(2,1)} %bitcast.8, bf16[3,32,256]{2,1,0:T(8,128)(2,1)} %bitcast.9, bf16[3,32,256]{2,1,0:T(8,128)(2,1)} %bitcast.10, s32[32,1]{1,0:T(8,128)} %copy.14.own_ref, s32[32,1]{1,0:T(8,128)} %copy.15.loc_ref, s32[2]{0:T(128)} %cnt_ref.1, ...), custom_call_target="tpu_custom_call" | custom-call | tf_op jit(solution)/shard_map/pallas_call | solution.py:357
  85.7 1.8 %copy.17 = bf16[32,3,2048]{2,0,1:T(8,128)(2,1)} copy(bf16[32,3,2048]{2,0,1:T(8,128)(2,1)} %bitcast.6) | data formatting | bytes 786432
Async XLA Ops:
  0.0 0.7 copy-start
  0.7 0.7 copy-start.1

commit v2 on v1

--- a/solution.py
+++ b/solution.py
@@ -12,6 +12,7 @@
 LOG2E = 1.4426950408889634
 LOW = -1e30
 GROUP = 8
+CHUNK = 4
 MESH = pl.DeviceIdType.MESH
 F32 = jnp.float32
 BF16 = jnp.bfloat16
@@ -42,9 +43,9 @@
     ck_hbm, cv_hbm, dk_hbm, dv_hbm, down_hbm, up_hbm,
     out_ref,
     ck, cv, dk, dv, down, up,
-    sx, rx, sb, rb, sq, rq, so, ro, part,
+    sx, rx, sb, rb, sq, rq, so, ro, sl, rl, part,
     delta, bias, lse, qh, own_out, own_lse,
-    in_sem, x_s, x_r, b_s, b_r, q_s, q_r, o_s, o_r, p_s, p_r,
+    in_sem, x_s, x_r, b_s, b_r, q_s, q_r, o_s, o_r, l_s, l_r, p_s, p_r,
 ):
     steps, reqs, width = x_ref.shape
     cols = b_ref.shape[2]
@@ -56,16 +57,22 @@
     ctx = ck.shape[1]
     total = n * rows
     home = steps * reqs
-    half = cols // kvs
     scale = LOG2E * HEAD ** -0.5
     me = lax.axis_index("batch")
     mt = lax.axis_index("tensor")
 
+    def partner(i):
+        to, bit = 0, 1
+        while bit < n:
+            to = to + bit * lax.rem(me // bit + i // bit, 2)
+            bit *= 2
+        return to
+
     barrier = pltpu.get_barrier_semaphore()
 
     @pl.loop(1, n)
     def _(i):
-        pl.semaphore_signal(barrier, inc=1, device_id={"batch": lax.rem(me + i, n)}, device_id_type=MESH)
+        pl.semaphore_signal(barrier, inc=1, device_id={"batch": partner(i)}, device_id_type=MESH)
 
     for i in range(1, tn):
         pl.semaphore_signal(barrier, inc=1, device_id={"tensor": lax.rem(mt + i, tn)}, device_id_type=MESH)
@@ -79,7 +86,9 @@
     for load in loads:
         load.start()
 
-    owner_col = own_ref[...]
+    diagonal = iota((reqs, reqs), 0) == iota((reqs, reqs), 1)
+    owner_col = jnp.sum(jnp.where(diagonal, own_ref[...], 0), axis=1, keepdims=True)
+    tenant_col = jnp.sum(jnp.where(diagonal, loc_ref[...], 0), axis=1, keepdims=True)
     wide_step, wide_req = split_index(iota((reqs, home), 1), reqs, steps)
     sub = iota((reqs, home), 0)
     owner_wide = jnp.sum(jnp.where(sub == wide_req, owner_col, 0), axis=0, keepdims=True)
@@ -93,7 +102,7 @@
     ).astype(BF16)
 
     tenant_tall = jnp.concatenate(
-        [jnp.broadcast_to(loc_ref[...].astype(F32), (reqs, HEAD))] * steps, axis=0
+        [jnp.broadcast_to(tenant_col.astype(F32), (reqs, HEAD))] * steps, axis=0
     ).astype(BF16)
     x_all = x_ref[...].reshape(home, width)
     sx[:, :, width:] = dot(pack, tenant_tall).reshape(n, rows, HEAD).astype(BF16)
@@ -101,14 +110,14 @@
         sx[:, :, c : c + 512] = dot(pack, x_all[:, c : c + 512]).reshape(n, rows, 512).astype(BF16)
 
     def copy(src, dst, ssem, rsem, i):
-        to = lax.rem(me + i, n)
+        to = partner(i)
         return pltpu.make_async_remote_copy(
             src_ref=src.at[to], dst_ref=dst.at[me], send_sem=ssem.at[i], recv_sem=rsem.at[i],
             device_id={"batch": to}, device_id_type=MESH,
         )
 
     def landed(src, dst, ssem, rsem, i):
-        come = lax.rem(me - i + n, n)
+        come = partner(i)
         pltpu.make_async_remote_copy(
             src_ref=src.at[come], dst_ref=dst.at[come], send_sem=ssem.at[i], recv_sem=rsem.at[i],
             device_id={"batch": come}, device_id_type=MESH,
@@ -118,17 +127,17 @@
     def start_all(*refs):
         @pl.loop(1, n)
         def _(i):
-            copy(*refs, i).start()
+            copy(*refs, n - i).start()
 
     def wait_all(*refs):
         @pl.loop(1, n)
         def _(i):
-            landed(*refs, i)
+            landed(*refs, n - i)
 
     def sent_all(*refs):
         @pl.loop(1, n)
         def _(i):
-            copy(*refs, i).wait_send()
+            copy(*refs, n - i).wait_send()
 
     def stacked(ref, lo, size):
         return jnp.concatenate(
@@ -142,8 +151,16 @@
     b_all = b_ref[...].reshape(home, cols)
     for c in range(0, cols, 512):
         sb[:, :, c : c + 512] = dot(pack, b_all[:, c : c + 512]).reshape(n, rows, 512).astype(BF16)
-    start_all(sb, rb, b_s, b_r)
+    copy(sb, rb, b_s, b_r, n - 1).start()
     rb[me] = sb[me]
+
+    @pl.loop(1, n)
+    def _(i):
+        copy(sx, rx, x_s, x_r, n - i).wait_send()
+
+        @pl.when(i > 1)
+        def _():
+            copy(sb, rb, b_s, b_r, n - i).start()
 
     loads[0].wait()
     wait_all(sx, rx, x_s, x_r)
@@ -197,23 +214,24 @@
 
     @pl.loop(1, n)
     def _(i):
-        j = landed(sb, rb, b_s, b_r, i)
+        j = landed(sb, rb, b_s, b_r, n - i)
         adapt(j)
-        pltpu.make_async_remote_copy(
-            src_ref=sq.at[j], dst_ref=rq.at[me], send_sem=q_s.at[n - i], recv_sem=q_r.at[n - i],
-            device_id={"batch": j}, device_id_type=MESH,
-        ).start()
+        copy(sq, rq, q_s, q_r, n - i).start()
 
     loads[2].wait()
     loads[3].wait()
     lane = iota((total, HEAD), 1)
     _, lane_head = split_index(lane, heads, HEAD // heads)
-    for k in range(kvs):
+    def chunk(c):
+        at = slice(c * CHUNK * HEAD, (c + 1) * CHUNK * HEAD)
+        return so.at[:, :, at], ro.at[:, :, at], o_s.at[c], o_r.at[c]
+
+    for c in range(heads // CHUNK):
+        k = c * CHUNK // per_kv
         mine = slice(k * HEAD, (k + 1) * HEAD)
 
-        @pl.loop(0, per_kv)
-        def _(g):
-            h = k * per_kv + g
+        @pl.loop(c * CHUNK, (c + 1) * CHUNK)
+        def _(h):
             at = pl.ds(pl.multiple_of(h * HEAD, HEAD), HEAD)
             q = delta[:, at].astype(BF16)
             keys = dk[:, :, mine].reshape(tenants * doc_len, HEAD)
@@ -225,7 +243,7 @@
             so[:, :, at] = mixed.reshape(n, rows, HEAD).astype(BF16)
             lse[...] = jnp.where(lane_head == h, peak + jnp.log2(amount), lse[...])
 
-        if k == kvs - 1:
+        if c == heads // CHUNK - 1:
             value = lse[...]
             first = value.astype(BF16).astype(F32)
             second = (value - first).astype(BF16).astype(F32)
@@ -234,11 +252,12 @@
                 lane < heads, first,
                 jnp.where(lane < 2 * heads, second, jnp.where(lane < 3 * heads, third, 0.0)),
             )
-            so[:, :, cols:] = pieces.reshape(n, rows, HEAD).astype(BF16)
-        lo, size = k * half, half + (HEAD if k == kvs - 1 else 0)
-        chunk = (so.at[:, :, lo : lo + size], ro.at[:, :, lo : lo + size], o_s.at[k], o_r.at[k])
-        start_all(*chunk)
-        ro[me, :, lo : lo + size] = so[me, :, lo : lo + size]
+            sl[...] = pieces.reshape(n, rows, HEAD).astype(BF16)
+            start_all(sl, rl, l_s, l_r)
+            rl[me] = sl[me]
+        start_all(*chunk(c))
+        at = slice(c * CHUNK * HEAD, (c + 1) * CHUNK * HEAD)
+        ro[me, :, at] = so[me, :, at]
 
     tall_step, tall_req = split_index(iota((home, total), 0), reqs, steps)
     owner_tall = jnp.concatenate([owner_col] * steps, axis=0)
@@ -294,32 +313,31 @@
                     iota((GROUP, HEAD), 1) == h, level[piece], own_lse[r, :]
                 )
 
-    for k in range(kvs):
-        lo, size = k * half, half + (HEAD if k == kvs - 1 else 0)
-        wait_all(so.at[:, :, lo : lo + size], ro.at[:, :, lo : lo + size], o_s.at[k], o_r.at[k])
+    wait_all(sl, rl, l_s, l_r)
     from_piece, from_head = split_index(iota((HEAD, HEAD), 0), heads, HEAD // heads)
     fold = jnp.where(
         (from_head == iota((HEAD, HEAD), 1)) & (from_piece < 3), 1.0, 0.0
     ).astype(BF16)
-    doc_lse = dot(dot(unpack, stacked(ro, cols, HEAD).astype(BF16)).astype(BF16), fold)
+    doc_lse = dot(dot(unpack, stacked(rl, 0, HEAD).astype(BF16)).astype(BF16), fold)
     top = jnp.maximum(doc_lse, own_lse[...])
     doc_part = jnp.exp2(doc_lse - top)
     own_part = jnp.exp2(own_lse[...] - top)
     alpha = doc_part / (doc_part + own_part)
-    for c in range(0, cols, 512):
-        doc = dot(unpack, stacked(ro, c, 512).astype(BF16))
-        for h in range(c // HEAD, (c + 512) // HEAD):
+    for c in range(heads // CHUNK):
+        wait_all(*chunk(c))
+        doc = dot(unpack, stacked(ro, c * CHUNK * HEAD, CHUNK * HEAD).astype(BF16))
+        for e in range(CHUNK):
+            h = c * CHUNK + e
             own = own_out[:, h * HEAD : (h + 1) * HEAD]
             weight = alpha[:, h : h + 1]
-            both = doc[:, h * HEAD - c : (h + 1) * HEAD - c] * weight + own * (1.0 - weight)
+            both = doc[:, e * HEAD : (e + 1) * HEAD] * weight + own * (1.0 - weight)
             out_ref[:, :, h * HEAD : (h + 1) * HEAD] = both.reshape(steps, reqs, HEAD).astype(BF16)
 
-    sent_all(sx, rx, x_s, x_r)
     sent_all(sb, rb, b_s, b_r)
     sent_all(sq, rq, q_s, q_r)
-    for k in range(kvs):
-        lo, size = k * half, half + (HEAD if k == kvs - 1 else 0)
-        sent_all(so.at[:, :, lo : lo + size], ro.at[:, :, lo : lo + size], o_s.at[k], o_r.at[k])
+    sent_all(sl, rl, l_s, l_r)
+    for c in range(heads // CHUNK):
+        sent_all(*chunk(c))
     for i in range(1, tn):
         part_copy(i).wait_send()
 
@@ -345,7 +363,6 @@
     tn = lax.axis_size("tensor")
     cap = max(2, 2 * reqs // n)
     rows = -(-cap * steps // 8) * 8
-    kvs = fresh_key_rows.shape[2] // HEAD
     tenants, rank, _ = adapter_down_panel.shape
     doc_len = document_key_rows.shape[1]
     total = n * rows
@@ -367,8 +384,8 @@
             )
         ]
         + [pltpu.VMEM((n, rows, width + HEAD), BF16)] * 2
-        + [pltpu.VMEM((n, rows, cols), BF16)] * 4
-        + [pltpu.VMEM((n, rows, cols + HEAD), BF16)] * 2
+        + [pltpu.VMEM((n, rows, cols), BF16)] * 6
+        + [pltpu.VMEM((n, rows, HEAD), BF16)] * 2
         + [
             pltpu.VMEM((tn, total, tenants * rank), F32),
             pltpu.VMEM((total, cols), F32),
@@ -380,7 +397,8 @@
             dma((6,)),
         ]
         + [dma((n,))] * 6
-        + [dma((kvs, n))] * 2
+        + [dma((cols // HEAD // CHUNK, n))] * 2
+        + [dma((n,))] * 2
         + [dma((tn,))] * 2,
         compiler_params=pltpu.CompilerParams(
             collective_id=0, has_side_effects=True, vmem_limit_bytes=56 * 2**20
@@ -390,8 +408,8 @@
         base_query_rows.transpose(1, 0, 2),
         fresh_key_rows.transpose(1, 0, 2),
         fresh_value_rows.transpose(1, 0, 2),
-        tenant_owner_batch,
-        tenant_local_index[:, None],
+        tenant_owner_batch.reshape(1, reqs),
+        tenant_local_index.reshape(1, reqs),
         document_block_count,
         context_key_cache,
         context_value_cache,

time: 87.7 us -> 82.7 us (0.943)
  Pallas kernels: 83.7 us -> 80.8 us
  local copies, waits for them, and re-layouts: 3.8 us -> 1.77 us
    pallas_call x1, Pallas kernels: 83.7 us -> 80.8 us  [local(): pl.pallas_call(functools.partial(kernel, n, tn, cap, rows), out_shape=jax...]
    unnamed x6 -> x1, local copies, waits for them, and re-layouts: 3.12 us -> 1.77 us
where the time goes in v2:
time: 82.7 us; the launch traced here: 82.5 us
  Pallas kernels  80.8 us (98%)
  local copies, waits for them, and re-layouts  1.77 us (2%)
    pallas_call x1, Pallas kernels, local(): pl.pallas_call(functools.partial(kernel, n, tn, cap, rows), out_shape=jax...  80.8 us
    unnamed x1, local copies, waits for them, and re-layouts  1.77 us

profile of v2, /device:TPU:0, one launch (start us, length us, event | category | flops | bytes accessed | tf_op | source)
XLA Modules:
  0.0 82.5 jit_solution(11497035499904159213)
XLA Ops:
  0.0 80.8 %shard_map.127 = bf16[3,32,2048]{2,1,0:T(8,128)(2,1)} custom-call(bf16[3,32,2048]{2,1,0:T(8,128)(2,1)} %bitcast.8, bf16[3,32,2048]{2,1,0:T(8,128)(2,1)} %bitcast.9, bf16[3,32,256]{2,1,0:T(8,128)(2,1)} %bitcast.10, bf16[3,32,256]{2,1,0:T(8,128)(2,1)} %bitcast.11, s32[1,32]{1,0:T(1,128)} %bitcast.12, s32[1,32]{1,0:T(1,128)} %bitcast.13, s32[2]{0:T(128)} %cnt_ref.1, ...), custom_call_target="tpu_custom_call" | custom-call | tf_op jit(solution)/shard_map/pallas_call | solution.py:374
  80.8 1.8 %copy.15 = bf16[32,3,2048]{2,0,1:T(8,128)(2,1)} copy(bf16[32,3,2048]{2,0,1:T(8,128)(2,1)} %bitcast.7) | data formatting | bytes 786432

commit v3 on v2

--- a/solution.py
+++ b/solution.py
@@ -35,6 +35,10 @@
 
 def dot_nt(a, b):
     return lax.dot_general(a, b, (((1,), (1,)), ((), ())), preferred_element_type=F32)
+
+
+def with_ones(values):
+    return jnp.concatenate([values, jnp.ones_like(values)], axis=1)
 
 
 def kernel(
@@ -151,7 +155,15 @@
     b_all = b_ref[...].reshape(home, cols)
     for c in range(0, cols, 512):
         sb[:, :, c : c + 512] = dot(pack, b_all[:, c : c + 512]).reshape(n, rows, 512).astype(BF16)
-    copy(sb, rb, b_s, b_r, n - 1).start()
+    half = cols // kvs
+
+    def part_of(src, dst, ssem, rsem, k):
+        at = slice(k * half, (k + 1) * half)
+        return src.at[:, :, at], dst.at[:, :, at], ssem.at[k], rsem.at[k]
+
+    base = [part_of(sb, rb, b_s, b_r, k) for k in range(kvs)]
+    query = [part_of(sq, rq, q_s, q_r, k) for k in range(kvs)]
+    copy(*base[0], n - 1).start()
     rb[me] = sb[me]
 
     @pl.loop(1, n)
@@ -160,7 +172,7 @@
 
         @pl.when(i > 1)
         def _():
-            copy(sb, rb, b_s, b_r, n - i).start()
+            copy(*base[0], n - i).start()
 
     loads[0].wait()
     wait_all(sx, rx, x_s, x_r)
@@ -188,6 +200,13 @@
         sees = (tenant_rows[:, :1] == float(t)) & (key < DOC_BLOCK * cnt_ref[t])
         bias[:, t * doc_len : (t + 1) * doc_len] = jnp.where(sees, 0.0, LOW)
     lse[...] = jnp.zeros_like(lse)
+
+    for k in range(1, kvs):
+
+        @pl.loop(1, n)
+        def _(i):
+            copy(*base[k - 1], n - i).wait_send()
+            copy(*base[k], n - i).start()
 
     loads[1].wait()
     for i in range(1, tn):
@@ -203,20 +222,21 @@
     for c in range(0, cols, 512):
         delta[:, c : c + 512] = dot(spread, up[:, :, c : c + 512].reshape(tenants * rank, 512))
 
-    def adapt(j):
-        here = pl.ds(pl.multiple_of(j * rows, 8), rows)
-        q = (rb[j].astype(F32) + delta[here, :]).astype(BF16)
-        sq[j] = q
-        delta[here, :] = q.astype(F32)
-
-    adapt(me)
-    rq[me] = sq[me]
-
-    @pl.loop(1, n)
-    def _(i):
-        j = landed(sb, rb, b_s, b_r, n - i)
-        adapt(j)
-        copy(sq, rq, q_s, q_r, n - i).start()
+    def adapt(j, k):
+        here, at = pl.ds(pl.multiple_of(j * rows, 8), rows), slice(k * half, (k + 1) * half)
+        q = (rb[j, :, at].astype(F32) + delta[here, at]).astype(BF16)
+        sq[j, :, at] = q
+        delta[here, at] = q.astype(F32)
+
+    def adapt_all(k):
+        adapt(me, k)
+        rq[me, :, k * half : (k + 1) * half] = sq[me, :, k * half : (k + 1) * half]
+
+        @pl.loop(1, n)
+        def _(i):
+            j = landed(*base[k], n - i)
+            adapt(j, k)
+            copy(*query[k], n - i).start()
 
     loads[2].wait()
     loads[3].wait()
@@ -229,19 +249,26 @@
     for c in range(heads // CHUNK):
         k = c * CHUNK // per_kv
         mine = slice(k * HEAD, (k + 1) * HEAD)
-
-        @pl.loop(c * CHUNK, (c + 1) * CHUNK)
-        def _(h):
+        if c * CHUNK % per_kv == 0:
+            adapt_all(k)
+
+        def attend(h):
             at = pl.ds(pl.multiple_of(h * HEAD, HEAD), HEAD)
             q = delta[:, at].astype(BF16)
             keys = dk[:, :, mine].reshape(tenants * doc_len, HEAD)
             s = dot_nt(q, keys) * scale + bias[...]
             peak = jnp.max(s, axis=1, keepdims=True)
             w = jnp.exp2(s - peak).astype(BF16)
-            amount = jnp.sum(w.astype(F32), axis=1, keepdims=True)
-            mixed = dot(w, dv[:, :, mine].reshape(tenants * doc_len, HEAD)) / amount
-            so[:, :, at] = mixed.reshape(n, rows, HEAD).astype(BF16)
+            mixed = dot(w, with_ones(dv[:, :, mine].reshape(tenants * doc_len, HEAD)))
+            amount = mixed[:, HEAD:]
+            doc = mixed[:, :HEAD] / amount
+            so[:, :, at] = doc.reshape(n, rows, HEAD).astype(BF16)
             lse[...] = jnp.where(lane_head == h, peak + jnp.log2(amount), lse[...])
+
+        @pl.loop(0, CHUNK // 2)
+        def _(g):
+            attend(c * CHUNK + 2 * g)
+            attend(c * CHUNK + 2 * g + 1)
 
         if c == heads // CHUNK - 1:
             value = lse[...]
@@ -270,7 +297,8 @@
     unpack = jnp.where(
         (slot_owner == owner_tall) & (slot_row == tall_step * cap + rank_tall), 1.0, 0.0
     ).astype(BF16)
-    wait_all(sq, rq, q_s, q_r)
+    for k in range(kvs):
+        wait_all(*query[k])
     for c in range(0, cols, 512):
         qh[:, c : c + 512] = dot(unpack, stacked(rq, c, 512).astype(BF16))
     own_lse[...] = jnp.zeros_like(own_lse)
@@ -301,11 +329,11 @@
             peak = jnp.maximum(jnp.max(sc, axis=1, keepdims=True), jnp.max(sf, axis=1, keepdims=True))
             wc = jnp.exp2(sc - peak).astype(BF16)
             wf = jnp.exp2(sf - peak).astype(BF16)
-            amount = jnp.sum(wc.astype(F32), axis=1, keepdims=True) + jnp.sum(
-                wf.astype(F32), axis=1, keepdims=True
-            )
-            mixed = (dot(wc, values) + dot(wf, fv_ref[:, :, mine].reshape(home, HEAD))) / amount
+            fresh_values = fv_ref[:, :, mine].reshape(home, HEAD)
+            mixed = dot(wc, with_ones(values)) + dot(wf, with_ones(fresh_values))
+            amount = mixed[:, HEAD:]
             level = peak + jnp.log2(amount)
+            mixed = mixed[:, :HEAD] / amount
             for e, (r, h) in enumerate(places):
                 piece = slice(e * GROUP, (e + 1) * GROUP)
                 own_out[r, h * HEAD : (h + 1) * HEAD] = mixed[piece]
@@ -333,8 +361,9 @@
             both = doc[:, e * HEAD : (e + 1) * HEAD] * weight + own * (1.0 - weight)
             out_ref[:, :, h * HEAD : (h + 1) * HEAD] = both.reshape(steps, reqs, HEAD).astype(BF16)
 
-    sent_all(sb, rb, b_s, b_r)
-    sent_all(sq, rq, q_s, q_r)
+    sent_all(*base[kvs - 1])
+    for k in range(kvs):
+        sent_all(*query[k])
     sent_all(sl, rl, l_s, l_r)
     for c in range(heads // CHUNK):
         sent_all(*chunk(c))
@@ -396,7 +425,8 @@
             pltpu.VMEM((home, HEAD), F32),
             dma((6,)),
         ]
-        + [dma((n,))] * 6
+        + [dma((n,))] * 2
+        + [dma((fresh_key_rows.shape[2] // HEAD, n))] * 4
         + [dma((cols // HEAD // CHUNK, n))] * 2
         + [dma((n,))] * 2
         + [dma((tn,))] * 2,

time: 82.7 us -> 83.1 us (level)
  no operation moved by 1% of the time
where the time goes in v3:
time: 83.1 us; the launch traced here: 82.9 us
  Pallas kernels  81.1 us (98%)
  local copies, waits for them, and re-layouts  1.77 us (2%)
    pallas_call x1, Pallas kernels, local(): pl.pallas_call(functools.partial(kernel, n, tn, cap, rows), out_shape=jax...  81.1 us
    unnamed x1, local copies, waits for them, and re-layouts  1.77 us

profile of v3, /device:TPU:0, one launch (start us, length us, event | category | flops | bytes accessed | tf_op | source)
XLA Modules:
  0.0 82.9 jit_solution(14154580443386379372)
XLA Ops:
  0.0 81.1 %shard_map.127 = bf16[3,32,2048]{2,1,0:T(8,128)(2,1)} custom-call(bf16[3,32,2048]{2,1,0:T(8,128)(2,1)} %bitcast.8, bf16[3,32,2048]{2,1,0:T(8,128)(2,1)} %bitcast.9, bf16[3,32,256]{2,1,0:T(8,128)(2,1)} %bitcast.10, bf16[3,32,256]{2,1,0:T(8,128)(2,1)} %bitcast.11, s32[1,32]{1,0:T(1,128)} %bitcast.12, s32[1,32]{1,0:T(1,128)} %bitcast.13, s32[2]{0:T(128)} %cnt_ref.1, ...), custom_call_target="tpu_custom_call" | custom-call | tf_op jit(solution)/shard_map/pallas_call | solution.py:403
  81.2 1.8 %copy.15 = bf16[32,3,2048]{2,0,1:T(8,128)(2,1)} copy(bf16[32,3,2048]{2,0,1:T(8,128)(2,1)} %bitcast.7) | data formatting | bytes 786432
